TPU v7x, 512 devices: a whole 4x8x8 slice. The times are simulated.
512 devices in a mesh: tm: 64 (over z_hi, y, x), head: 8 (over z_lo, core).
Axes of the slice: x: 4, y: 8, z: 8 (z_hi: 2, z_lo: 4; z = z_hi * 4 + z_lo), core: 2. Of those that a mesh axis runs over, the one named last changes fastest.
Arguments:
- frames_in: bfloat16 [64, 1024, 1024], P('tm', 'head'), may hold values from -400 to 400
- in_weight: bfloat16 [1024, 5120], P('tm', 'head'), may hold values from -0.1875 to 0.1875
- out_weight: bfloat16 [1024, 1024], replicated, may hold values from -0.1875 to 0.1875
- block_ids: int32 [1024], replicated, may hold values from 0 to 15, as said below
- block_lists: int32 [16, 4], replicated, may hold values from 0 to 15, as said below
- decays: float32 [64, 16, 16], P('tm', 'head'), may hold values from 0.3 to 1
Outputs:
- layer_out: bfloat16 [64, 1024, 1024], P('tm', 'head')
Inputs may be any that keep to these rules, and one draw needn't show every extreme that they name: `block_ids`: each of the 16 block ids is held by exactly 64 tokens. `block_lists`: row g starts with g itself, followed by 4 - 1 further blocks, all different.
All inputs are finite; a program needn't handle non-finite values.
Results may differ from a plain program's by a relative error of at most 0.0069.
Values may be sent and summed in bfloat16 or wider, within the bound.
A program may use at most 128 MiB of HBM per device.

v0:
```python
import math
import jax
import jax.numpy as jnp
from jax import lax
from jax.sharding import PartitionSpec as P

HD = 64
N = 64
TOKS = 1024
NB = 16
epsilon = 1e-06


def carried_in(shard, axis, combine, identity):
    peers, index = (lax.axis_size(axis), lax.axis_index(axis))
    everything = jax.tree.map(lambda part: lax.all_gather(part, axis), shard)
    start = jax.tree.map(
        lambda part, zero: jnp.broadcast_to(jnp.asarray(zero, part.dtype), part.shape),
        shard,
        identity,
    )

    def step(k, before):
        reached = k < index
        new = combine(before, jax.tree.map(lambda part: part[k], everything))
        return jax.tree.map(lambda a, b: jnp.where(reached, a, b), new, before)

    return lax.fori_loop(0, peers, step, start)


def head_norm(values):
    wide = values.astype(jnp.float32)
    return (wide * lax.rsqrt(jnp.mean(wide * wide, axis=-1, keepdims=True) + epsilon)).astype(
        jnp.bfloat16
    )


def combine(earlier, after_it):
    return (earlier[0] * after_it[0], after_it[0][:, :, None] * earlier[1] + after_it[1])


def body(frames_in, in_weight, out_weight, block_ids, block_lists, decays):
    frame_count, local_tokens, feature_width = frames_in.shape
    heads_here = decays.shape[1]
    groups = decays.shape[2]
    tokens = block_ids.shape[0]
    block_size = tokens // groups
    head_size = HD
    state_size = N
    selected_count = block_lists.shape[1]
    inputs_wide = frames_in.astype(jnp.float32)
    normed = (
        inputs_wide
        * lax.rsqrt(jnp.mean(inputs_wide * inputs_wide, axis=-1, keepdims=True) + epsilon)
    ).astype(jnp.bfloat16)
    full_rows = lax.all_gather(in_weight, "tm", axis=0, tiled=True)
    flat_rows = normed.reshape(frame_count * local_tokens, feature_width)
    local_flat = jnp.dot(
        flat_rows,
        lax.all_gather(full_rows, "head", axis=1, tiled=True),
        preferred_element_type=jnp.float32,
    ).astype(jnp.bfloat16)
    local_proj = local_flat.reshape(frame_count, local_tokens, local_flat.shape[1])
    projected = lax.all_to_all(local_proj, "head", split_axis=2, concat_axis=1, tiled=True)
    projected = projected.reshape(frame_count, tokens, heads_here, 5, head_size)
    sort_order = jnp.argsort(block_ids, stable=True)
    inverse_order = jnp.argsort(sort_order, stable=True)
    sorted_proj = jnp.take(projected, sort_order, axis=1).reshape(
        frame_count, groups, block_size, heads_here, 5, head_size
    )
    queries = head_norm(sorted_proj[:, :, :, :, 0])
    key_rows = head_norm(sorted_proj[:, :, :, :, 1])
    values_sorted = sorted_proj[:, :, :, :, 2]
    map_sorted = sorted_proj[:, :, :, :, 3, :state_size]
    readers_sorted = sorted_proj[:, :, :, :, 4, :state_size].astype(jnp.float32)
    chosen_keys = jnp.take(key_rows, block_lists, axis=1).reshape(
        frame_count, groups, selected_count * block_size, heads_here, head_size
    )
    chosen_values = jnp.take(values_sorted, block_lists, axis=1).reshape(
        frame_count, groups, selected_count * block_size, heads_here, head_size
    )
    updates = jnp.einsum(
        "fgshn,fgshd->fhgnd", map_sorted, values_sorted, preferred_element_type=jnp.float32
    )
    local_state = jnp.zeros((heads_here, groups, state_size, head_size), jnp.float32)
    running = jnp.ones((heads_here, groups), jnp.float32)
    frame_at = 0
    local_state = decays[frame_at][:, :, None, None] * local_state + updates[frame_at]
    running = decays[frame_at] * running
    states = [local_state]
    products = [running]
    identity = (
        jnp.ones((heads_here, groups), jnp.float32),
        jnp.zeros((heads_here, groups, state_size * head_size), jnp.float32),
    )
    carried = carried_in(
        (running, local_state.reshape(heads_here, groups, state_size * head_size)),
        "tm",
        combine,
        identity,
    )
    incoming = carried[1].reshape(heads_here, groups, state_size, head_size)
    ssm_scale = 1.0 / (N * math.sqrt(TOKS // NB))
    frame_at = 0
    full_state = states[frame_at] + products[frame_at][:, :, None, None] * incoming
    readout_sorted = (
        jnp.einsum(
            "gshn,hgnd->gshd", readers_sorted[frame_at], full_state, precision=lax.Precision.HIGHEST
        )
        * ssm_scale
    )
    scores = jnp.einsum(
        "gshd,guhd->hgsu",
        queries[frame_at],
        chosen_keys[frame_at],
        preferred_element_type=jnp.float32,
    ) / math.sqrt(head_size)
    exponent = jnp.exp(scores)
    weights = (exponent / jnp.sum(exponent, axis=-1, keepdims=True)).astype(jnp.bfloat16)
    attended = jnp.einsum(
        "hgsu,guhd->gshd", weights, chosen_values[frame_at], preferred_element_type=jnp.float32
    )
    mixed_sorted = (
        (attended + readout_sorted).astype(jnp.bfloat16).reshape(tokens, heads_here * head_size)
    )
    frames_mixed = [jnp.take(mixed_sorted, inverse_order, axis=0)]
    mixed = jnp.stack(frames_mixed, axis=0)
    token_mix = lax.all_to_all(mixed, "head", split_axis=1, concat_axis=2, tiled=True)
    result = jnp.dot(
        token_mix.reshape(frame_count * local_tokens, token_mix.shape[2]),
        out_weight,
        preferred_element_type=jnp.float32,
    )
    return result.astype(jnp.bfloat16).reshape(frame_count, local_tokens, feature_width)


def solution(mesh):
    return jax.shard_map(
        body,
        mesh=mesh,
        in_specs=(P("tm", "head", None), P("tm", "head"), P(), P(), P(), P("tm", "head", None)),
        out_specs=P("tm", "head", None),
        check_vma=False,
    )
```

profile of v0, /device:TPU:1, one launch (start us, length us, event | category | flops | bytes accessed | tf_op | source)
XLA Modules:
  0.0 990.8 jit_solution(7445949897962662394)
XLA Ops:
  7.3 138.0 %all-gather.4.cloned.1.call-done = bf16[1024,640]{1,0:T(8,128)(2,1)} async-done(((bf16[16,640]{1,0:T(8,128)(2,1)}), bf16[1024,640]{1,0:T(8,128)(2,1)}) %all-gather.4.cloned.1.call-update) | async-done | bytes 1310736 | tf_op jit(solution)/shard_map/all_gather | solution.py:56
  146.4 112.3 %all-gather.6.cloned.1.call-done = bf16[1024,5120]{1,0:T(8,128)(2,1)} async-done(((bf16[1024,640]{1,0:T(8,128)(2,1)}), bf16[1024,5120]{1,0:T(8,128)(2,1)}) %all-gather.6.cloned.1.call-update) | async-done | bytes 10485776 | tf_op jit(solution)/shard_map/all_gather | solution.py:60
  258.7 5.7 fusion.1
  264.4 4.1 copy.51
  269.1 28.9 %reduce.4 = bf16[5120,128]{1,0:T(8,128)(2,1)S(1)} reduce(bf16[5120,1,128]{2,1,0:T(2,128)(2,1)} %bitcast.84, bf16[]{:T(256)} %broadcast.155), dimensions={1}, to_apply=%bitcast.66.reduce_sub_computation | reduce | bytes 2621442
  299.2 6.9 all-to-all-start
  306.1 4.4 sort.31
  310.6 26.9 %all-to-all-done = bf16[8,2,40960]{2,1,0:T(2,128)(2,1)S(1)} async-done(((bf16[8,2,40960]{2,1,0:T(2,128)(2,1)}), bf16[8,2,40960]{2,1,0:T(2,128)(2,1)S(1)}, u32[]{:S(2)}, u32[]{:S(2)}) %all-to-all-start) | async-done | bytes 1310752 | tf_op jit(solution)/shard_map/all_to_all | solution.py:64
  337.5 3.7 reshape.273
  345.4 6.2 copy.53
  351.6 13.9 %gather_fusion = bf16[1024,2,5,64]{3,1,2,0:T(2,128)(2,1)} fusion(bf16[1024,2,5,64]{3,1,2,0:T(2,128)(2,1)} %copy.53, s32[1024]{0:T(1024)S(1)} %fusion.28), kind=kCustom, calls=%fused_computation.2 | custom fusion | bytes 2625536 | tf_op jit(solution)/shard_map/jit(_take)/gather | solution.py:68
  373.2 4.4 sort.32
  377.6 194.0 %all_gather.14 = f32[64,2,16]{2,1,0:T(2,128)S(1)} all-gather(f32[1,2,16]{2,1,0:T(2,128)S(1)} %copy-done.4), channel_id=1, replica_groups=mesh['tm'=64,'head'=8] {'tm'}, dimensions={0}, use_global_device_ids=true | all-gather | bytes 8320 | tf_op jit(solution)/shard_map/all_gather | solution.py:16
  580.7 4.7 broadcast_select_fusion.1
  585.4 4.3 copy.59
  589.7 4.3 squeeze_reshape.7
  594.0 4.3 copy.56
  598.3 4.3 squeeze_reshape.6
  608.0 273.5 %all-gather.8.cloned.1.call-done = f32[64,2,16,4096]{3,2,1,0:T(8,128)} async-done(((f32[1,2,16,4096]{3,2,1,0:T(8,128)}), f32[64,2,16,4096]{3,2,1,0:T(8,128)}) %all-gather.8.cloned.1.call-update) | async-done | bytes 33554448 | tf_op jit(solution)/shard_map/all_gather | solution.py:16
  881.5 77.4 %while.14 = (s32[]{:T(128)}, f32[2,16,4096]{2,1,0:T(8,128)S(1)}, s32[]{:T(128)}, f32[64,2,16]{2,1,0:T(2,128)S(1)}, f32[64,2,16,4096]{3,2,1,0:T(8,128)}, /*index=5*/s32[]{:T(128)}, s32[]{:T(128)}) while((s32[]{:T(128)}, f32[2,16,4096]{2,1,0:T(8,128)S(1)}, s32[]{:T(128)}, f32[64,2,16]{2,1,0:T(2,128)S(1)}, ...), condition=%wide.region_7.9_spmd.clone, body=%wide.region_6.8_spmd.clone.sunk | while | flops 524292 | bytes 1573353 | solution.py:28
  960.3 3.2 fusion.5
  964.2 3.2 gather_fusion.1
  968.0 2.3 reduce.5
  970.3 12.2 %all_to_all.30 = bf16[8,2,8192]{2,1,0:T(2,128)(2,1)S(1)} all-to-all(bf16[8,2,8192]{2,1,0:T(2,128)(2,1)S(1)} %reshape.274), channel_id=1, replica_groups=mesh['tm'=64,'head'=8] {'head'}, dimensions={0} | all-to-all | bytes 524288 | tf_op jit(solution)/shard_map/all_to_all | solution.py:128
  (195 shorter events, 109.9 us)
Async XLA Ops:
  6.5 976.5 %copy-start = (bf16[1024,1024]{1,0:T(8,128)(2,1)S(1)}, bf16[1024,1024]{1,0:T(8,128)(2,1)}, u32[]{:S(2)}) copy-start(bf16[1024,1024]{1,0:T(8,128)(2,1)} %param.12) | copy-start | bytes 6291460
  6.5 138.8 %all-gather.4.cloned.1.call-start = ((), (), s32[]{:S(2)}) async-start(), calls=%async_computation.2 | async-start | bytes 1331200 | tf_op jit(solution)/shard_map/all_gather | solution.py:56
  7.3 251.5 %all-gather.6.cloned.1.call-start = ((), (), s32[]{:S(2)}) async-start(), calls=%async_computation.3 | async-start | bytes 11796480 | tf_op jit(solution)/shard_map/all_gather | solution.py:60
  298.0 8.2 copy-start.6
  298.0 12.6 %copy-start.4 = (f32[1,2,16]{2,1,0:T(2,128)S(1)}, f32[1,2,16]{2,1,0:T(2,128)}, u32[]{:S(2)}) copy-start(f32[1,2,16]{2,1,0:T(2,128)} %param.15) | copy-start | bytes 388
  299.2 38.3 %all-to-all-start = ((bf16[8,2,40960]{2,1,0:T(2,128)(2,1)}), bf16[8,2,40960]{2,1,0:T(2,128)(2,1)S(1)}, u32[]{:S(2)}, u32[]{:S(2)}) async-start(bf16[8,2,40960]{2,1,0:T(2,128)(2,1)} %reshape.272), calls=%async_computation | async-start | bytes 2621440 | tf_op jit(solution)/shard_map/all_to_all | solution.py:64
  306.1 575.3 %all-gather.8.cloned.1.call-start = ((), (), s32[]{:S(2)}) async-start(), calls=%async_computation.4 | async-start | bytes 34078720 | tf_op jit(solution)/shard_map/all_gather | solution.py:16
  367.9 1.4 copy-start.1
  369.7 3.1 copy-start.2
  369.7 3.1 copy-start.5
  602.6 3.6 copy-start.3
Sparse Core Ops, SparseCore 0:
  11.9 133.4 all-gather.3
  147.4 111.2 all-gather.5
  373.0 508.4 all-gather.7
where the time goes:
time: 995 us; the launch traced here: 991 us
  waiting for transfers between devices  551 us (55%)
  blocking collectives  206 us (21%)
  other arithmetic  127 us (13%)
  local copies, waits for them, and re-layouts  69.2 us (7%)
  matrix products  14.2 us (1%)
  between operations  13.4 us (1%)
    all_gather x1, waiting for transfers between devices, carried_in(): everything = jax.tree.map(lambda part: lax.all_gather(part, axis), shard)  273 us
    all_gather x1, blocking collectives, carried_in(): everything = jax.tree.map(lambda part: lax.all_gather(part, axis), shard)  194 us
    all_gather x1, waiting for transfers between devices, body(): full_rows = lax.all_gather(in_weight, 'tm', axis=0, tiled=True)  138 us
    all_gather x1, waiting for transfers between devices, body(): lax.all_gather(full_rows, 'head', axis=1, tiled=True)  112 us
    select_n x64, other arithmetic, step(): return jax.tree.map(lambda a, b: jnp.where(reached, a, b), new, before)  74.9 us
    unnamed x3, other arithmetic  31.2 us
    all_to_all x1, waiting for transfers between devices, body(): lax.all_to_all(local_proj, 'head', split_axis=2, concat_axis=1, tiled=True)  26.9 us
  transfers between devices with their start and end apart: 4, of which 4 were waited for; matrix products, arithmetic and copies ran while one was open for 5% of the time, Pallas kernels for 0%

commit v1 on v0

--- a/solution.py
+++ b/solution.py
@@ -61,7 +61,15 @@
         preferred_element_type=jnp.float32,
     ).astype(jnp.bfloat16)
     local_proj = local_flat.reshape(frame_count, local_tokens, local_flat.shape[1])
-    projected = lax.all_to_all(local_proj, "head", split_axis=2, concat_axis=1, tiled=True)
+    projected = jnp.concatenate(
+        lax.all_to_all(
+            jnp.stack(jnp.split(local_proj, lax.axis_size("head"), axis=2)),
+            "head",
+            split_axis=0,
+            concat_axis=0,
+        ),
+        axis=1,
+    )
     projected = projected.reshape(frame_count, tokens, heads_here, 5, head_size)
     sort_order = jnp.argsort(block_ids, stable=True)
     inverse_order = jnp.argsort(sort_order, stable=True)

time: 995 us -> 960 us (0.965)
  other arithmetic: 127 us -> 98.4 us
    unnamed x3 -> x2, other arithmetic: 31.2 us -> 2.21 us
    reshape x3 -> x0, local copies, waits for them, and re-layouts: 11.7 us -> none  [the longest x2 7.63 us: body(): projected = projected.reshape(frame_count, tokens, heads_here, 5, head_size)]
where the time goes in v1:
time: 960 us; the launch traced here: 956 us
  waiting for transfers between devices  551 us (57%)
  blocking collectives  206 us (21%)
  other arithmetic  98.4 us (10%)
  local copies, waits for them, and re-layouts  63.6 us (7%)
  matrix products  14.2 us (1%)
  between operations  13.4 us (1%)
    all_gather x1, waiting for transfers between devices, carried_in(): everything = jax.tree.map(lambda part: lax.all_gather(part, axis), shard)  273 us
    all_gather x1, blocking collectives, carried_in(): everything = jax.tree.map(lambda part: lax.all_gather(part, axis), shard)  194 us
    all_gather x1, waiting for transfers between devices, body(): full_rows = lax.all_gather(in_weight, 'tm', axis=0, tiled=True)  138 us
    all_gather x1, waiting for transfers between devices, body(): lax.all_gather(full_rows, 'head', axis=1, tiled=True)  112 us
    select_n x64, other arithmetic, step(): return jax.tree.map(lambda a, b: jnp.where(reached, a, b), new, before)  74.9 us
    all_to_all x1, waiting for transfers between devices, body(): lax.all_to_all(jnp.stack(jnp.split(local_proj, lax.axis_size('head'), axi...  26.9 us
  transfers between devices with their start and end apart: 4, of which 4 were waited for; matrix products, arithmetic and copies ran while one was open for 5% of the time, Pallas kernels for 0%

profile of v1, /device:TPU:1, one launch (start us, length us, event | category | flops | bytes accessed | tf_op | source)
XLA Modules:
  0.0 956.2 jit_solution(715328489524011374)
XLA Ops:
  7.3 138.0 %all-gather.4.cloned.1.call-done = bf16[1024,640]{1,0:T(8,128)(2,1)} async-done(((bf16[16,640]{1,0:T(8,128)(2,1)}), bf16[1024,640]{1,0:T(8,128)(2,1)}) %all-gather.4.cloned.1.call-update) | async-done | bytes 1310736 | tf_op jit(solution)/shard_map/all_gather | solution.py:56
  146.4 112.3 %all-gather.6.cloned.1.call-done = bf16[1024,5120]{1,0:T(8,128)(2,1)} async-done(((bf16[1024,640]{1,0:T(8,128)(2,1)}), bf16[1024,5120]{1,0:T(8,128)(2,1)}) %all-gather.6.cloned.1.call-update) | async-done | bytes 10485776 | tf_op jit(solution)/shard_map/all_gather | solution.py:60
  258.7 5.7 fusion.1
  269.8 6.9 all-to-all-start
  276.7 4.4 sort.31
  281.2 26.9 %all-to-all-done = bf16[8,1,128,640]{3,2,1,0:T(8,128)(2,1)S(1)} async-done(((bf16[8,1,128,640]{3,2,1,0:T(8,128)(2,1)}), bf16[8,1,128,640]{3,2,1,0:T(8,128)(2,1)S(1)}, u32[]{:S(2)}, u32[]{:S(2)}) %all-to-all-start) | async-done | bytes 1310752 | tf_op jit(solution)/shard_map/all_to_all | solution.py:65
  309.9 2.4 reshape.228
  312.3 4.2 copy.67
  316.5 13.9 %gather_fusion = bf16[1024,2,5,64]{3,1,2,0:T(2,128)(2,1)} fusion(bf16[1024,2,5,64]{3,1,2,0:T(2,128)(2,1)} %copy.67, s32[1024]{0:T(1024)S(1)} %fusion.36), kind=kCustom, calls=%fused_computation.2 | custom fusion | bytes 2625536 | tf_op jit(solution)/shard_map/jit(_take)/gather | solution.py:76
  330.3 2.1 copy.68
  337.8 4.4 sort.32
  342.5 194.3 %all_gather.14 = f32[64,2,16]{2,1,0:T(2,128)S(1)} all-gather(f32[1,2,16]{2,1,0:T(2,128)S(1)} %copy-done.4), channel_id=1, replica_groups=mesh['tm'=64,'head'=8] {'tm'}, dimensions={0}, use_global_device_ids=true | all-gather | bytes 8320 | tf_op jit(solution)/shard_map/all_gather | solution.py:16
  543.7 2.2 gather_fusion.2
  545.9 4.7 broadcast_select_fusion.1
  550.6 4.3 copy.73
  554.9 4.3 squeeze_reshape.7
  559.2 4.3 copy.70
  563.5 4.3 squeeze_reshape.6
  573.1 273.2 %all-gather.8.cloned.1.call-done = f32[64,2,16,4096]{3,2,1,0:T(8,128)} async-done(((f32[1,2,16,4096]{3,2,1,0:T(8,128)}), f32[64,2,16,4096]{3,2,1,0:T(8,128)}) %all-gather.8.cloned.1.call-update) | async-done | bytes 33554448 | tf_op jit(solution)/shard_map/all_gather | solution.py:16
  846.4 77.4 %while.14 = (s32[]{:T(128)}, f32[2,16,4096]{2,1,0:T(8,128)S(1)}, s32[]{:T(128)}, f32[64,2,16]{2,1,0:T(2,128)S(1)}, f32[64,2,16,4096]{3,2,1,0:T(8,128)}, /*index=5*/s32[]{:T(128)}, s32[]{:T(128)}) while((s32[]{:T(128)}, f32[2,16,4096]{2,1,0:T(8,128)S(1)}, s32[]{:T(128)}, f32[64,2,16]{2,1,0:T(2,128)S(1)}, ...), condition=%wide.region_7.9_spmd.clone, body=%wide.region_6.8_spmd.clone.sunk | while | flops 524292 | bytes 1573353 | solution.py:28
  925.2 3.2 fusion.5
  929.1 3.2 gather_fusion.1
  933.5 2.2 reduce.4
  935.8 12.2 %all_to_all.20 = bf16[8,2,8192]{2,1,0:T(2,128)(2,1)S(1)} all-to-all(bf16[8,2,8192]{2,1,0:T(2,128)(2,1)S(1)} %reshape.267), channel_id=1, replica_groups=mesh['tm'=64,'head'=8] {'head'}, dimensions={0} | all-to-all | bytes 524288 | tf_op jit(solution)/shard_map/all_to_all | solution.py:136
  (197 shorter events, 107.4 us)
Async XLA Ops:
  6.5 941.9 %copy-start = (bf16[1024,1024]{1,0:T(8,128)(2,1)S(1)}, bf16[1024,1024]{1,0:T(8,128)(2,1)}, u32[]{:S(2)}) copy-start(bf16[1024,1024]{1,0:T(8,128)(2,1)} %param.12) | copy-start | bytes 6291460
  6.5 138.8 %all-gather.4.cloned.1.call-start = ((), (), s32[]{:S(2)}) async-start(), calls=%async_computation.2 | async-start | bytes 1331200 | tf_op jit(solution)/shard_map/all_gather | solution.py:56
  7.3 251.5 %all-gather.6.cloned.1.call-start = ((), (), s32[]{:S(2)}) async-start(), calls=%async_computation.3 | async-start | bytes 11796480 | tf_op jit(solution)/shard_map/all_gather | solution.py:60
  266.4 10.3 %copy-start.6 = (s32[1024]{0:T(1024)S(1)}, s32[1024]{0:T(1024)}, u32[]{:S(2)}) copy-start(s32[1024]{0:T(1024)} %param.13) | copy-start | bytes 12292
  266.4 14.8 %copy-start.4 = (f32[1,2,16]{2,1,0:T(2,128)S(1)}, f32[1,2,16]{2,1,0:T(2,128)}, u32[]{:S(2)}) copy-start(f32[1,2,16]{2,1,0:T(2,128)} %param.15) | copy-start | bytes 388
  269.8 38.3 %all-to-all-start = ((bf16[8,1,128,640]{3,2,1,0:T(8,128)(2,1)}), bf16[8,1,128,640]{3,2,1,0:T(8,128)(2,1)S(1)}, u32[]{:S(2)}, u32[]{:S(2)}) async-start(bf16[8,1,128,640]{3,2,1,0:T(8,128)(2,1)} %fusion.27), calls=%async_computation | async-start | bytes 2621440 | tf_op jit(solution)/shard_map/all_to_all | solution.py:65
  276.7 569.7 %all-gather.8.cloned.1.call-start = ((), (), s32[]{:S(2)}) async-start(), calls=%async_computation.4 | async-start | bytes 34078720 | tf_op jit(solution)/shard_map/all_gather | solution.py:16
  332.8 1.4 copy-start.1
  334.6 3.1 copy-start.2
  334.6 7.5 copy-start.5
  567.8 3.6 copy-start.3
Sparse Core Ops, SparseCore 0:
  11.9 133.4 all-gather.3
  147.4 111.2 all-gather.5
  337.9 508.4 all-gather.7
